TPU v7x, 32 devices: a whole 2x2x4 slice. The times are simulated.
32 devices in a mesh: row: 4 (over z), col: 8 (over y, x, core).
Axes of the slice: x: 2, y: 2, z: 4, core: 2. Of those that a mesh axis runs over, the one named last changes fastest.
Arguments:
- front_diag: float32 [1024, 1024], replicated, may hold values from -4 to 16, as said below
- panel_rows: float32 [16384, 1024], P(('row', 'col')), may hold values from -1.2 to 1.2
- trailing: float32 [16384, 16384], P('row', 'col'), may hold values from -6 to 6
- pattern: int32 [64, 64], P('row', 'col'), may hold values 0 or 1
Outputs:
- diag_factor: float32 [1024, 1024], replicated
- panel_factor: float32 [16384, 1024], P(('row', 'col'))
- schur: float32 [16384, 16384], P('row', 'col')
Inputs may be any that keep to these rules, and one draw needn't show every extreme that they name: front_diag is symmetric and positive definite, with smallest eigenvalue at least 0.5.
All inputs are finite; a program needn't handle non-finite values. No bound on the sum of `pattern` on one device may be relied on, other than what follows from the above.
Results may differ from a plain program's by a relative error of at most 0.0003.
Values sent between devices are 32-bit elements; how exact they have to be, the bound alone decides.
No kernel may reach another device: no remote copies, remote signals or barrier semaphores. Data moves between devices by JAX's collectives and lax.ppermute only.
A program may use at most 192 MiB of HBM per device.

v0:
```python
import jax
import jax.numpy as jnp
from jax import lax
from jax.sharding import PartitionSpec as P

BLOCK = 256


def spread(block, axis, holder):
    block = jnp.where(lax.axis_index(axis) == holder, block, jnp.zeros_like(block))
    return lax.psum(block, axis)


def column_rows(row_part, col_rows):
    ratio = lax.axis_size("col") // lax.axis_size("row")
    offset = lax.axis_index("col") % ratio * col_rows
    return lax.dynamic_slice_in_dim(row_part, offset, col_rows, 0)


def local(front_diag, panel_rows, trailing, pattern):
    diag_factor = jnp.linalg.cholesky(front_diag)
    panel_factor = jax.scipy.linalg.solve_triangular(diag_factor, panel_rows.T, lower=True).T
    local_rows = trailing.shape[0]
    col_rows = trailing.shape[1]
    ratio = lax.axis_size("col") // lax.axis_size("row")
    root_row = lax.axis_index("col") // ratio
    row_part = lax.all_gather(panel_factor, "col", axis=0, tiled=True)
    piece = column_rows(row_part, col_rows)
    col_part = spread(piece, "row", root_row)
    update = jnp.dot(row_part, col_part.T, precision=lax.Precision.HIGHEST)
    row_blocks = local_rows // BLOCK
    col_blocks = col_rows // BLOCK
    row_index = lax.axis_index("row") * row_blocks + jnp.arange(row_blocks)
    col_index = lax.axis_index("col") * col_blocks + jnp.arange(col_blocks)
    lower = (row_index[:, None] >= col_index[None, :]).astype(jnp.float32)
    keep = pattern.astype(jnp.float32) * lower
    masked = update.reshape(row_blocks, BLOCK, col_blocks, BLOCK) * keep[:, None, :, None]
    schur = trailing - masked.reshape(local_rows, col_rows)
    return (diag_factor, panel_factor, schur)


def solution(mesh):
    return jax.shard_map(
        local,
        mesh=mesh,
        in_specs=(P(), P(("row", "col"), None), P("row", "col"), P("row", "col")),
        out_specs=(P(), P(("row", "col"), None), P("row", "col")),
        check_vma=False,
    )
```

profile of v0, /device:TPU:10, one launch (start us, length us, event | category | flops | bytes accessed | tf_op | source)
XLA Modules:
  0.0 868.4 jit_solution(10399720475324147559)
XLA Ops:
  7.2 5.3 copy.7
  12.6 4.4 fusion
  17.0 2.0 copy-done
  19.0 11.7 %cholesky.223 = f32[128,128]{1,0:T(8,128)S(1)} custom-call(f32[128,128]{1,0:T(8,128)S(1)} %cholesky.580), custom_call_target="Cholesky" | custom-call | tf_op jit(solution)/shard_map/jit(cholesky)/cholesky | solution.py:21
  30.8 9.8 %custom-call.63 = f32[1,128,128]{1,2,0:T(8,128)S(1)} custom-call(f32[1,128,128]{2,1,0:T(8,128)S(1)} %get-tuple-element.72), custom_call_target="InvertDiagBlocksLowerTriangular" | custom-call | tf_op jit(solution)/shard_map/jit(cholesky)/cholesky | solution.py:21
  40.6 2.5 cholesky.255
  43.1 2.3 constant_dynamic-update-slice_fusion.32
  45.4 1.5 convolution_subtract_fusion
  47.0 12.0 %cholesky.244 = f32[128,128]{1,0:T(8,128)S(1)} custom-call(f32[128,128]{1,0:T(8,128)S(1)} %cholesky.584), custom_call_target="Cholesky" | custom-call | tf_op jit(solution)/shard_map/jit(cholesky)/cholesky | solution.py:21
  59.7 9.8 %custom-call.64 = f32[1,128,128]{1,2,0:T(8,128)S(1)} custom-call(f32[1,128,128]{2,1,0:T(8,128)S(1)} %get-tuple-element.69), custom_call_target="InvertDiagBlocksLowerTriangular" | custom-call | tf_op jit(solution)/shard_map/jit(cholesky)/cholesky | solution.py:21
  69.5 1.2 convolution_dynamic-update-slice_fusion
  70.7 2.1 convolution_subtract_fusion.1
  72.8 11.7 %cholesky.468 = f32[128,128]{1,0:T(8,128)S(1)} custom-call(f32[128,128]{1,0:T(8,128)S(1)} %cholesky.589), custom_call_target="Cholesky" | custom-call | tf_op jit(solution)/shard_map/jit(cholesky)/cholesky | solution.py:21
  85.8 9.8 %custom-call.65 = f32[1,128,128]{1,2,0:T(8,128)S(1)} custom-call(f32[1,128,128]{2,1,0:T(8,128)S(1)} %get-tuple-element.66), custom_call_target="InvertDiagBlocksLowerTriangular" | custom-call | tf_op jit(solution)/shard_map/jit(cholesky)/cholesky | solution.py:21
  95.6 1.1 convolution_dynamic-update-slice_fusion.1
  96.8 2.3 convolution_subtract_fusion.2
  99.1 11.8 %cholesky.487 = f32[128,128]{1,0:T(8,128)S(1)} custom-call(f32[128,128]{1,0:T(8,128)S(1)} %cholesky.594), custom_call_target="Cholesky" | custom-call | tf_op jit(solution)/shard_map/jit(cholesky)/cholesky | solution.py:21
  111.6 0.7 compare_reduce_fusion.4
  112.3 9.8 %custom-call.66 = f32[1,128,128]{1,2,0:T(8,128)S(1)} custom-call(f32[1,128,128]{2,1,0:T(8,128)S(1)} %get-tuple-element.63), custom_call_target="InvertDiagBlocksLowerTriangular" | custom-call | tf_op jit(solution)/shard_map/jit(cholesky)/cholesky | solution.py:21
  122.1 1.1 convolution_dynamic-update-slice_fusion.3
  123.2 2.3 convolution_subtract_fusion.10
  125.5 11.7 %cholesky.506 = f32[128,128]{1,0:T(8,128)S(1)} custom-call(f32[128,128]{1,0:T(8,128)S(1)} %cholesky.599), custom_call_target="Cholesky" | custom-call | tf_op jit(solution)/shard_map/jit(cholesky)/cholesky | solution.py:21
  137.9 0.7 compare_reduce_fusion.3
  138.6 10.0 %custom-call.67 = f32[1,128,128]{1,2,0:T(8,128)S(1)} custom-call(f32[1,128,128]{2,1,0:T(8,128)S(1)} %get-tuple-element.60), custom_call_target="InvertDiagBlocksLowerTriangular" | custom-call | tf_op jit(solution)/shard_map/jit(cholesky)/cholesky | solution.py:21
  148.6 1.0 convolution_dynamic-update-slice_fusion.4
  149.6 2.3 convolution_subtract_fusion.11
  151.9 11.7 %cholesky.526 = f32[128,128]{1,0:T(8,128)S(1)} custom-call(f32[128,128]{1,0:T(8,128)S(1)} %cholesky.604), custom_call_target="Cholesky" | custom-call | tf_op jit(solution)/shard_map/jit(cholesky)/cholesky | solution.py:21
  164.2 0.7 compare_reduce_fusion.2
  164.9 9.8 %custom-call.68 = f32[1,128,128]{1,2,0:T(8,128)S(1)} custom-call(f32[1,128,128]{2,1,0:T(8,128)S(1)} %get-tuple-element.57), custom_call_target="InvertDiagBlocksLowerTriangular" | custom-call | tf_op jit(solution)/shard_map/jit(cholesky)/cholesky | solution.py:21
  174.7 0.9 convolution_dynamic-update-slice_fusion.5
  175.6 2.1 convolution_subtract_fusion.12
  177.7 12.1 %cholesky.546 = f32[128,128]{1,0:T(8,128)S(1)} custom-call(f32[128,128]{1,0:T(8,128)S(1)} %cholesky.609), custom_call_target="Cholesky" | custom-call | tf_op jit(solution)/shard_map/jit(cholesky)/cholesky | solution.py:21
  191.1 9.8 %custom-call.69 = f32[1,128,128]{1,2,0:T(8,128)S(1)} custom-call(f32[1,128,128]{2,1,0:T(8,128)S(1)} %get-tuple-element.54), custom_call_target="InvertDiagBlocksLowerTriangular" | custom-call | tf_op jit(solution)/shard_map/jit(cholesky)/cholesky | solution.py:21
  200.9 0.8 convolution_dynamic-update-slice_fusion.6
  201.7 1.8 convolution_subtract_fusion.13
  203.5 11.7 %cholesky.564 = f32[128,128]{1,0:T(8,128)S(1)} custom-call(f32[128,128]{1,0:T(8,128)S(1)} %convolution_subtract_fusion.13), custom_call_target="Cholesky" | custom-call | tf_op jit(solution)/shard_map/jit(cholesky)/cholesky | solution.py:21
  222.0 6.8 fusion.1
  228.8 22.5 %while.1 = (s32[]{:T(128)}, f32[1024,1024]{1,0:T(8,128)}, s32[8,2]{0,1:T(2,128)S(1)}, f32[8,128,128]{2,1,0:T(8,128)S(1)}, s32[]{:T(128)}) while((s32[]{:T(128)}, f32[1024,1024]{1,0:T(8,128)}, s32[8,2]{0,1:T(2,128)S(1)}, f32[8,128,128]{2,1,0:T(8,128)S(1)}, s32[]{:T(128)}) %tuple.63), condition=%wide.while_cond, body=%wide.while_body.sunk | while | flops 2 | bytes 131189 | solution.py:22
  229.4 2.2 bitcast_dynamic-update-slice_fusion.2
  232.3 2.2 bitcast_dynamic-update-slice_fusion.2
  235.1 2.2 bitcast_dynamic-update-slice_fusion.2
  237.9 2.2 bitcast_dynamic-update-slice_fusion.2
  240.7 2.2 bitcast_dynamic-update-slice_fusion.2
  243.5 2.2 bitcast_dynamic-update-slice_fusion.2
  246.4 2.2 bitcast_dynamic-update-slice_fusion.2
  249.2 2.1 bitcast_dynamic-update-slice_fusion.2
  251.3 78.8 %custom-call.70 = f32[8,128,128]{1,2,0:T(8,128)S(1)} custom-call(f32[8,128,128]{2,1,0:T(8,128)S(1)} %get-tuple-element.10), custom_call_target="InvertDiagBlocksLowerTriangular" | custom-call | tf_op jit(solution)/shard_map/jit(_solve_triangular)/triangular_solve | solution.py:22
  330.1 1.4 constant_dynamic-update-slice_fusion.17
  331.6 1.7 convolution_subtract_fusion.6
  333.8 2.0 convolution_subtract_fusion.5
  336.3 2.5 convolution_subtract_fusion.8
  339.3 2.8 convolution_subtract_fusion.9
  342.5 3.2 convolution_subtract_fusion.4
  346.2 3.6 convolution_subtract_fusion.7
  350.3 4.3 convolution_subtract_fusion.3
  355.0 1.3 copy-done.1
  356.4 91.1 %all-gather.2.cloned.1.call-done = f32[4096,1024]{0,1:T(8,128)} async-done(((f32[512,1024]{0,1:T(8,128)}), f32[4096,1024]{0,1:T(8,128)}) %all-gather.2.cloned.1.call-update) | async-done | bytes 16777232 | tf_op jit(solution)/shard_map/all_gather | solution.py:27
  447.5 8.2 dynamic-slice_select_fusion
  455.7 1.6 copy-done.2
  457.3 1.8 copy.9
  459.3 2.8 mul.27
  462.1 20.7 %copy.10 = f32[512,8,8,256]{3,1,2,0:T(8,128)} copy(f32[512,8,8,256]{3,2,1,0:T(8,128)S(1)} %bitcast.108) | data formatting | bytes 67108864
  482.8 262.1 %all-reduce.3.cloned.1.call-done = f32[2048,1024]{0,1:T(8,128)} async-done(((f32[2048,1024]{0,1:T(8,128)}), f32[2048,1024]{0,1:T(8,128)}) %all-reduce.3.cloned.1.call-update) | async-done | bytes 8388624 | tf_op jit(solution)/shard_map/psum | solution.py:11
  744.8 116.3 %multiply_subtract_fusion = f32[4096,2048]{1,0:T(8,128)} fusion(f32[4096,2048]{1,0:T(8,128)} %param.6, f32[4096,2048]{1,0:T(8,128)} %bitcast.109, f32[4096,1024]{0,1:T(8,128)} %all-gather.2.cloned.1.call-done, f32[2048,1024]{0,1:T(8,128)} %all-reduce.3.cloned.1.call-done), kind=kOutput, calls=%fused_computation.2 | convolution fusion | flops 103095992320 | bytes 125829120 | tf_op jit(solution)/shard_map/dot_general | solution.py:30
  (60 shorter events, 15.3 us)
Async XLA Ops:
  7.2 440.3 %all-gather.2.cloned.1.call-start = ((), (), s32[]{:S(2)}) async-start(), calls=%async_computation | async-start | bytes 18874368 | tf_op jit(solution)/shard_map/all_gather | solution.py:27
  17.0 2.0 copy-start
  331.6 7.7 copy-start.3
  355.0 1.3 copy-start.1
  356.4 388.5 %all-reduce.3.cloned.1.call-start = ((), (), s32[]{:S(2)}) async-start(), calls=%async_computation.1 | async-start | bytes 16777216 | tf_op jit(solution)/shard_map/psum | solution.py:11
  455.7 1.6 copy-start.2
  457.3 1.8 copy-start.4
Sparse Core Ops, SparseCore 0:
  356.5 90.9 all-gather.1
  455.9 288.9 all-reduce.2
where the time goes:
time: 882 us; the launch traced here: 868 us
  waiting for transfers between devices  353 us (40%)
  other arithmetic  271 us (31%)
  matrix products  164 us (19%)
  local copies, waits for them, and re-layouts  60.6 us (7%)
  between operations  19.8 us (2%)
    psum x1, waiting for transfers between devices, spread(): return lax.psum(block, axis)  262 us
    another operation x30, other arithmetic, local(): diag_factor = jnp.linalg.cholesky(front_diag)  172 us
    dot_general x1, matrix products, local(): update = jnp.dot(row_part, col_part.T, precision=lax.Precision.HIGHEST)  116 us
    all_gather x1, waiting for transfers between devices, local(): row_part = lax.all_gather(panel_factor, 'col', axis=0, tiled=True)  91.1 us
    another operation x3, other arithmetic, local(): jax.scipy.linalg.solve_triangular(diag_factor, panel_rows.T, lower=True)  85.6 us
    unnamed x13, local copies, waits for them, and re-layouts  32.7 us
    another operation x15, matrix products, local(): jax.scipy.linalg.solve_triangular(diag_factor, panel_rows.T, lower=True)  24.8 us
    another operation x14, matrix products, local(): diag_factor = jnp.linalg.cholesky(front_diag)  22.9 us
  transfers between devices with their start and end apart: 2, of which 2 were waited for; matrix products, arithmetic and copies ran while one was open for 3% of the time, Pallas kernels for 0%

commit v1 on v0

v1 whole, which is shorter than its diff:
```python
import functools

import jax
import jax.numpy as jnp
import numpy as np
from jax import lax
from jax.experimental import pallas as pl
from jax.experimental.pallas import tpu as pltpu
from jax.sharding import PartitionSpec as P

BLOCK = 256
T = 128
HIGHEST = lax.Precision.HIGHEST
AXES = ("row", "col")
F32, BF16 = jnp.float32, jnp.bfloat16


def tdot(a, b, precision=HIGHEST):
    return lax.dot_general(a, b, (((0,), (0,)), ((), ())), precision=precision, preferred_element_type=F32)


def split2(x):
    hi = x.astype(BF16)
    return hi, (x - hi.astype(F32)).astype(BF16)


def gram8(p):
    h = p.astype(BF16).astype(F32)
    m = (p - h).astype(BF16).astype(F32)
    l = p - h - m
    a = jnp.concatenate([h, h, m, m, h, l], 0).astype(BF16)
    b = jnp.concatenate([h, m, h, m, l, h], 0).astype(BF16)
    return tdot(a, b, None)


def factor_block(d):
    n = len(d)
    lane = lax.broadcasted_iota(jnp.int32, (8, T), 1)
    sub = lax.broadcasted_iota(jnp.int32, (8, T), 0)
    ws, us = [], []
    for g in range(n):
        e = d[g]
        cs = [jnp.broadcast_to(e[:, 8 * g + k : 8 * g + k + 1], (8, T)) for k in range(8)]
        inside = (lane >= 8 * g) & (lane < 8 * g + 8)
        e = jnp.where(inside, jnp.where(lane - 8 * g == sub, 1.0, 0.0), e)
        piv = jnp.ones((8, T), F32)
        for j in range(8):
            p = jnp.broadcast_to(cs[j][j : j + 1], (8, T))
            piv = jnp.where(sub == j, p, piv)
            if j == 7:
                break
            m = jnp.where(sub > j, cs[j] * (1.0 / p), 0.0)
            for k in range(j + 1, 8):
                cs[k] = cs[k] - m * jnp.broadcast_to(cs[k][j : j + 1], (8, T))
            e = e - m * jnp.broadcast_to(e[j : j + 1], (8, T))
        r = lax.rsqrt(piv)
        r = r * (1.5 - 0.5 * piv * r * r)
        e = e * r
        u = jnp.zeros((8, T), F32)
        for k in range(8):
            u = jnp.where((lane == 8 * g + k) & (sub <= k), cs[k] * r, u)
        us.append(jnp.where(lane >= 8 * g + 8, e, u))
        ws.append(jnp.where(lane < 8 * g + 8, e, 0.0))
        if g + 1 < n:
            update = gram8(e)
            for i in range(g + 1, n):
                d[i] = jnp.where(inside, 0.0, d[i]) - update[8 * i : 8 * i + 8]
    return ws, us


def factor_kernel(a_ref, old_ref, l_ref, inv_ref, new_ref, s_ref, w_ref, u_ref, p_ref, stage, sem):
    n = a_ref.shape[0]
    nb = n // T
    share = old_ref.shape[0] // nb

    def load(b):
        rows = pl.ds(pl.multiple_of(b * share, share), share)
        return pltpu.make_async_copy(old_ref.at[rows], stage.at[lax.rem(b, 2)], sem.at[lax.rem(b, 2)])

    def store(b):
        rows = pl.ds(pl.multiple_of(b * share, share), share)
        return pltpu.make_async_copy(stage.at[lax.rem(b, 2)], new_ref.at[rows], sem.at[2 + lax.rem(b, 2)])

    load(0).start()
    s_ref[...] = a_ref[...]
    l_ref[...] = jnp.zeros_like(l_ref)
    inv_ref[...] = jnp.zeros_like(inv_ref)
    colb = lax.broadcasted_iota(jnp.int32, (T, n), 1) // T

    @pl.loop(0, nb)
    def _(b):
        load(b).wait()
        store(b).start()

        @pl.when(b + 1 < nb)
        def _():
            @pl.when(b >= 1)
            def _():
                store(b - 1).wait()

            load(b + 1).start()

        here = pl.ds(pl.multiple_of(b * T, T), T)
        block = s_ref[here, here]
        ws, us = factor_block([block[8 * g : 8 * g + 8] for g in range(T // 8)])
        for g in range(T // 8):
            w_ref[8 * g : 8 * g + 8, :] = ws[g]
            u_ref[8 * g : 8 * g + 8, :] = us[g]
        w = w_ref[...]
        p_ref[...] = jnp.dot(w, s_ref[here, :], precision=HIGHEST, preferred_element_type=F32)
        p_ref[:, here] = w
        inv_ref[here, :] = jnp.where(colb <= b, p_ref[...], 0.0)
        l_ref[here, here] = u_ref[...].T

        @pl.loop(b + 1, nb)
        def _(i):
            there = pl.ds(pl.multiple_of(i * T, T), T)
            ui = p_ref[:, there]
            s_ref[there, :] = jnp.where(colb == b, 0.0, s_ref[there, :]) - tdot(ui, p_ref[...])
            l_ref[there, here] = ui.T

    if nb > 1:
        store(nb - 2).wait()
    store(nb - 1).wait()


VMEM = pl.BlockSpec(memory_space=pltpu.VMEM)
ANY = pl.BlockSpec(memory_space=pl.ANY)
BIG = pltpu.CompilerParams(vmem_limit_bytes=58 << 20)


def cost(flops, moved):
    return pl.CostEstimate(flops=int(flops), bytes_accessed=int(moved), transcendentals=0)


def factor(a, old):
    n = a.shape[0]
    full = jax.ShapeDtypeStruct((n, n), F32)
    return pl.pallas_call(
        factor_kernel,
        out_shape=(full, full, jax.ShapeDtypeStruct(old.shape, F32)),
        in_specs=[VMEM, ANY],
        out_specs=(VMEM, VMEM, ANY),
        scratch_shapes=[
            pltpu.VMEM((n, n), F32),
            pltpu.VMEM((T, T), F32),
            pltpu.VMEM((T, T), F32),
            pltpu.VMEM((T, n), F32),
            pltpu.VMEM((2, old.shape[0] * T // n, old.shape[1]), F32),
            pltpu.SemaphoreType.DMA((4,)),
        ],
        compiler_params=BIG,
        cost_estimate=cost(8e10, 12 << 20),
        name="factor",
    )(a, old)


def dot3(a_hi, a_lo, b_hi, b_lo):
    dot = functools.partial(jnp.dot, preferred_element_type=F32)
    return dot(a_hi, b_hi) + dot(a_lo, b_hi) + dot(a_hi, b_lo)


def inverse_kernel(inv_ref, rows_ref, x_ref, cat_ref, lt_hi, lt_lo, in_hi, in_lo, r_hi, r_lo):
    n = inv_ref.shape[0]

    @pl.loop(0, n // T)
    def _(k):
        part = pl.ds(pl.multiple_of(k * T, T), T)
        v = inv_ref[part, :]
        in_hi[part, :], in_lo[part, :] = split2(v)
        lt_hi[:, part], lt_lo[:, part] = split2(v.T)

    r_hi[...], r_lo[...] = split2(rows_ref[...])
    step = min(n, 256)
    for j in range(n // step):
        cols, deep = slice(j * step, (j + 1) * step), slice(0, (j + 1) * step)
        x_ref[:, cols] = dot3(r_hi[:, deep], r_lo[:, deep], lt_hi[deep, cols], lt_lo[deep, cols])
    for i in range(n // step):
        rows, deep = slice(i * step, (i + 1) * step), slice(i * step, n)
        cat_ref[rows, :], cat_ref[n + i * step : n + (i + 1) * step, :] = split2(dot3(lt_hi[rows, deep], lt_lo[rows, deep], in_hi[deep, :], in_lo[deep, :]))


def inverse(inv, rows):
    n, m = inv.shape[0], rows.shape[0]
    return pl.pallas_call(
        inverse_kernel,
        out_shape=(jax.ShapeDtypeStruct((m, n), F32), jax.ShapeDtypeStruct((2 * n, n), BF16)),
        in_specs=[VMEM] * 2,
        out_specs=(VMEM,) * 2,
        scratch_shapes=[pltpu.VMEM((n, n), BF16)] * 4 + [pltpu.VMEM((m, n), BF16)] * 2,
        compiler_params=BIG,
        cost_estimate=cost(8 * n * n * n, 16 << 20),
        name="inverse",
    )(inv, rows)


def pick_kernel(layout, info, *refs):
    arrays, outs, (buf, in_sem, out_sem) = refs[: layout["arrays"]], refs[layout["arrays"] : -3], refs[-3:]
    moves, at = [], 0
    for out, segments in zip(outs, layout["segments"]):
        for to, size, choices, entry in segments:
            moves.append((out, to, size, choices, entry, at))
            at += size
    for wait in (False, True):
        for number, (out, to, size, choices, entry, at) in enumerate(moves):
            stage = buf.at[pl.ds(at, size)]
            store = pltpu.make_async_copy(stage, out.at[pl.ds(to, size)], out_sem.at[number])
            for n, (frm, off) in enumerate(choices):
                load = pltpu.make_async_copy(arrays[frm].at[pl.ds(off, size)], stage, in_sem.at[number])

                @pl.when(True if entry is None else info[entry] == n)
                def _(load=load, store=store):
                    if wait:
                        load.wait()
                        store.start()
                    else:
                        load.start()
    for number, (out, to, size, choices, entry, at) in enumerate(moves):
        store = pltpu.make_async_copy(buf.at[pl.ds(at, size)], out.at[pl.ds(to, size)], out_sem.at[number])

        @pl.when(True if entry is None else info[entry] >= 0)
        def _(store=store):
            store.wait()


def pick(info, arrays, segments):
    cols = arrays[0].shape[1]
    count = sum(map(len, segments))
    return pl.pallas_call(
        functools.partial(pick_kernel, dict(arrays=len(arrays), segments=segments)),
        out_shape=tuple(jax.ShapeDtypeStruct((sum(s[1] for s in seg), cols), F32) for seg in segments),
        grid_spec=pltpu.PrefetchScalarGridSpec(
            num_scalar_prefetch=1,
            grid=(1,),
            in_specs=[ANY] * len(arrays),
            out_specs=(ANY,) * len(segments),
            scratch_shapes=[
                pltpu.VMEM((sum(s[1] for seg in segments for s in seg), cols), F32),
                pltpu.SemaphoreType.DMA((count,)),
                pltpu.SemaphoreType.DMA((count,)),
            ],
        ),
        compiler_params=BIG,
        cost_estimate=cost(1000, 1000),
        name="pick",
    )(info, *arrays)


AHEAD, RING, SLOTS, GROUP = 4, 12, 4, 4


def update_kernel(layout, info, pattern, *refs):
    pieces, parts, tiles = (layout[k] for k in ("pieces", "parts", "tiles"))
    tile, sub, part = (layout[k] for k in ("tile", "sub", "part"))
    keeps_rows, gives, near = layout["keeps_rows"], layout["gives"], layout["near"]
    refs = list(refs)
    take = lambda k: [refs.pop(0) for _ in range(k)]
    sources = [take(p["sources"]) for p in pieces]
    ready = [take(1)[0] if p["ready"] is not None else None for p in pieces]
    part_refs, cat_ref = take(len(parts)), take(1)[0]
    take(1 + layout["rows_in"])
    out, rows_hbm, given = take(1)[0], (take(layout["rows_any"]) or [None])[0], (take(1 if gives else 0) or [None])[0]
    cat, p_buf, ht, row_f32, rows_v, block, flat, sem, p_sem, ht_sem, f32_sem, row_sem, in_sem, out_sem = refs
    count, steps = len(pieces), len(tiles)
    buffer = [sum(p["fresh"] for p in pieces[:m]) for m in range(count)]
    width, n = p_buf.shape[1:]
    subs = width // sub
    each = count * subs
    rb, cb = out.shape[0] // BLOCK, out.shape[1] // BLOCK
    r, c, diag = info[0], info[1], info[3] == 1

    def row_of(step):
        at = step * tile
        return (jnp.bitwise_xor(at // part, c) * part) + at % part

    def col_of(m, s):
        q = info[pieces[0]["number"]]
        for k in range(1, count):
            q = jnp.where(m == k, info[pieces[k]["number"]], q)
        return q * width + s * sub

    def place(t):
        e = flat[t]
        return e // each, (e % each) // subs, e % subs

    def view(t):
        step, m, s = place(t)
        row, col = pl.multiple_of(row_of(step), tile), pl.multiple_of(col_of(m, s), sub)
        return out.at[pl.ds(row, tile), pl.ds(col, sub)]

    def load(t):
        return pltpu.make_async_copy(view(t), block.at[lax.rem(t, RING)], in_sem.at[lax.rem(t, RING)])

    def store(t):
        return pltpu.make_async_copy(block.at[lax.rem(t, RING)], view(t), out_sem.at[lax.rem(t, RING)])

    def prefetch(t, total):
        @pl.when(t < total)
        def _():
            @pl.when(t >= RING)
            def _():
                store(t - RING).wait()

            load(t).start()

    def every(copies, what):
        for yes, copy in copies:
            if yes is True:
                getattr(copy, what)()
            else:
                @pl.when(yes)
                def _(copy=copy):
                    getattr(copy, what)()

    @pl.when(info[layout["needed"]] == 1)
    def _():
        copy = pltpu.make_async_copy
        cats = [(True, copy(cat_ref, cat, sem.at[0]))]
        loads = [[] for _ in pieces]
        for m, p in enumerate(pieces):
            for k in range(p["sources"]):
                chosen = (info[p["where"]] == k) if p["sources"] > 1 else True
                loads[m].append((jnp.logical_not(diag) & chosen, copy(sources[m][k], p_buf.at[buffer[m]], p_sem.at[m, k])))
            if p["fresh"]:
                for k, (mask, off, size, frm) in enumerate(parts):
                    to = p_buf.at[buffer[m], pl.ds(off, size)]
                    loads[m].append((diag & (info[p["mask"]] == mask), copy(part_refs[k].at[pl.ds(frm, size)], to, p_sem.at[m, 2 + k])))
        hts = []
        for m, p in enumerate(pieces):
            if p["ready"] is not None:
                src = ready[m].at[pl.ds(p["ready"] * width, width)]
                yes = jnp.logical_not(diag) if p["fresh"] else True
                hts.append((yes, copy(src, ht.at[m], ht_sem.at[m])))
        stored = [t for t, (k, _) in enumerate(tiles) if k is None]
        floats = [t for t, (k, _) in enumerate(tiles) if k is not None]
        rows = [(True, copy(rows_hbm.at[pl.ds(t * tile, tile)], rows_v.at[pl.ds(t * tile, tile)], row_sem.at[t])) for t in stored]

        def float_copy(u):
            k, off = tiles[floats[u]]
            return copy(part_refs[k].at[pl.ds(off, tile)], row_f32.at[u % SLOTS], f32_sem.at[u % SLOTS])

        def keep_copy(u):
            here = pl.ds(floats[u] * tile, tile)
            return copy(rows_v.at[here], rows_hbm.at[here], row_sem.at[floats[u]])

        for m in range(count):
            every(loads[m], "start")
        every(cats, "start")

        def note(e, found):
            step, m, s = e // each, (e % each) // subs, e % subs
            row, col = row_of(step) // BLOCK, col_of(m, s) // BLOCK
            flat[found] = e
            kept = (pattern[row, col] == 1) & (r * rb + row >= c * cb + col)
            if near:
                now = step >= near
                for k, p in enumerate(pieces):
                    now = now | ((m == k) & (diag if p["ready"] is not None else True)) if p["fresh"] else now
                kept = kept & now
            return found + kept.astype(jnp.int32)

        total = lax.fori_loop(0, steps * each, note, 0)
        for t in range(AHEAD):
            prefetch(t, total)

        step = min(width, 256)
        chunks = [(m, at) for m, p in enumerate(pieces) if p["fresh"] for at in range(0, width, step)]
        gone = []
        for number, (m, at) in enumerate(chunks):
            if at == 0:
                every(loads[m], "wait")
            if number == 0:
                every(cats, "wait")
                for u in range(min(SLOTS, len(floats))):
                    float_copy(u).start()
                every(rows, "start")
                every(hts, "start")
            here = slice(at, at + step)

            def multiply(m=m, here=here):
                hi, lo = split2(p_buf[buffer[m], here])
                ht[m, here, :n], ht[m, here, n:] = split2(dot3(hi, lo, cat[:n], cat[n:]))

            if pieces[m]["ready"] is None:
                multiply()
            else:
                pl.when(diag)(multiply)
            if gives and at + step == width:
                gone.append((True, copy(ht.at[m], given.at[pl.ds(m * width, width)], sem.at[1 + m])))
                every(gone[-1:], "start")
            share = [u for u in range(len(floats)) if u * len(chunks) // len(floats) == number]
            for u in share:
                float_copy(u).wait()
                rows_at = pl.ds(floats[u] * tile, tile)
                rows_v[rows_at, :n], rows_v[rows_at, n:] = split2(row_f32[u % SLOTS])
                if u + SLOTS < len(floats):
                    float_copy(u + SLOTS).start()
                if keeps_rows:
                    keep_copy(u).start()
        every(hts, "wait")
        every(rows, "wait")

        def product(t):
            tile_at, m, s = place(t)
            mine = rows_v[pl.ds(pl.multiple_of(tile_at * tile, tile), tile), :]
            cols = pl.ds(pl.multiple_of(s * sub, sub), sub)
            dot = functools.partial(lax.dot_general, dimension_numbers=(((1,), (1,)), ((), ())), preferred_element_type=F32)
            return dot(mine[:, :n], ht[m, cols, :n]) + dot(mine[:, n:], ht[m, cols, :n]) + dot(mine[:, :n], ht[m, cols, n:])

        def finish(t, value):
            load(t).wait()
            block[lax.rem(t, RING)] = block[lax.rem(t, RING)] - value
            store(t).start()

        def work(t, size):
            for k in range(size):
                prefetch(t + k + AHEAD, total)
            values = [product(t + k) for k in range(size)]
            for k in range(size):
                finish(t + k, values[k])

        whole = total // GROUP * GROUP

        @pl.loop(0, whole, step=GROUP)
        def _(t):
            work(t, GROUP)

        @pl.loop(whole, total)
        def _(t):
            work(t, 1)

        @pl.loop(jnp.maximum(total - RING, 0), total)
        def _(t):
            store(t).wait()

        every(gone, "wait")
        if keeps_rows:
            for u in range(len(floats)):
                keep_copy(u).wait()


def update(info, pattern, pieces, parts, tiles, near, needed, tile, part, cat, schur, rows, keeps_rows, gives):
    n = cat.shape[1]
    width = next(p[3][0].shape[0] for p in pieces if p[3])
    local_rows, local_cols = schur.shape
    sub = min(width, BLOCK)
    count, steps = len(pieces), len(tiles)
    layout = dict(
        pieces=[
            dict(number=a, mask=b, where=w, sources=len(x), ready=None if y is None else y[1], fresh=b is not None)
            for a, b, w, x, y in pieces
        ],
        parts=[(mask, off, size, frm) for mask, off, size, _, frm in parts],
        tiles=tiles,
        near=near,
        needed=needed,
        tile=tile,
        sub=sub,
        part=part,
        keeps_rows=keeps_rows,
        gives=gives,
        rows_in=0 if rows is None else 1,
        rows_any=1 if keeps_rows or rows is not None else 0,
    )
    operands = [x for p in pieces for x in p[3]] + [p[4][0] for p in pieces if p[4] is not None] + [p[3] for p in parts] + [cat, schur]
    aliases = {2 + len(operands) - 1: 0}
    shapes = [jax.ShapeDtypeStruct(schur.shape, F32)]
    if rows is not None:
        operands.append(rows)
        aliases[2 + len(operands) - 1] = 1
    if layout["rows_any"]:
        shapes.append(jax.ShapeDtypeStruct((local_rows, 2 * n), BF16))
    if gives:
        shapes.append(jax.ShapeDtypeStruct((count * width, 2 * n), BF16))
    dma = pltpu.SemaphoreType.DMA
    return pl.pallas_call(
        functools.partial(update_kernel, layout),
        out_shape=tuple(shapes),
        grid_spec=pltpu.PrefetchScalarGridSpec(
            num_scalar_prefetch=2,
            grid=(1,),
            in_specs=[ANY] * len(operands),
            out_specs=(ANY,) * len(shapes),
            scratch_shapes=[
                pltpu.VMEM((2 * n, n), BF16),
                pltpu.VMEM((sum(p["fresh"] for p in layout["pieces"]), width, n), F32),
                pltpu.VMEM((count, width, 2 * n), BF16),
                pltpu.VMEM((SLOTS, tile, n), F32),
                pltpu.VMEM((steps * tile, 2 * n), BF16),
                pltpu.VMEM((RING, tile, sub), F32),
                pltpu.SMEM((steps * count * (width // sub) + 1,), jnp.int32),
                dma((2 + count,)),
                dma((count, 2 + len(parts))),
                dma((count,)),
                dma((SLOTS,)),
                dma((steps,)),
                dma((RING,)),
                dma((RING,)),
            ],
        ),
        input_output_aliases=aliases,
        compiler_params=BIG,
        cost_estimate=cost(1000, 1000),
        name="update",
    )(info, pattern, *operands)


def plan(nrow, ncol):
    half, ratio = nrow // 2, ncol // nrow
    if (nrow, ncol) != (4, 8):
        shift = {nrow - 1: 0, nrow - 2: half}
        free = [g for g in range(1, nrow) if g != half]
        for i in range(nrow - 2):
            shift[i] = free[i]
        rounds = [{} for _ in range(nrow)]
        for m in range(nrow):
            for i in range(nrow):
                for j in range(i * ratio):
                    q = m ^ shift[i]
                    rounds[m][i, j] = (divmod(j * nrow + q, ncol), "own", q)
        return rounds
    rounds = [{} for _ in range(4)]

    def at(z, y, x, k):
        return z, (y * 2 + x) * 2 + k

    def put(m, to, frm, kind, x, k):
        rounds[m][at(*to)] = (at(*frm), kind, 2 * x + k)

    first = {0: (0, 1), 1: (0, 0), 2: (1, 0)}
    for z in (1, 2, 3):
        for src in range(z):
            y, x = divmod(src, 2)
            for core in (0, 1):
                half_x = first[src][core] if z != 2 else 1 - first[src][core]
                for m in (0, 1):
                    k = m if z != 1 else 1 - m
                    put(m, (z, y, x, core), (src, core, half_x, k), "own", half_x, k)
    put(2, (3, 0, 0, 0), (0, 0, 0, 0), "x", 1, 0)
    put(2, (3, 0, 0, 1), (0, 0, 0, 1), "y", 0, 1)
    put(3, (3, 0, 0, 0), (0, 0, 0, 1), "x", 1, 1)
    put(3, (3, 0, 0, 1), (0, 1, 1, 0), "x", 0, 0)
    put(2, (3, 0, 1, 0), (1, 0, 1, 0), "own", 1, 0)
    put(2, (3, 0, 1, 1), (1, 0, 1, 1), "y", 1, 1)
    put(3, (3, 0, 1, 0), (1, 0, 1, 1), "own", 1, 1)
    put(3, (3, 0, 1, 1), (1, 1, 1, 0), "own", 1, 0)
    put(2, (3, 1, 0, 1), (2, 1, 0, 0), "x", 1, 0)
    put(2, (3, 1, 0, 0), (2, 1, 0, 1), "y", 0, 1)
    put(3, (3, 1, 0, 1), (2, 1, 1, 1), "own", 1, 1)
    put(3, (3, 1, 0, 0), (2, 1, 0, 0), "y", 0, 0)
    put(2, (2, 0, 0, 0), (3, 0, 0, 0), "a", 0, 0)
    put(3, (2, 0, 0, 0), (3, 0, 0, 0), "b", 0, 1)
    put(2, (2, 0, 0, 1), (3, 0, 0, 1), "a", 1, 0)
    put(3, (2, 0, 0, 1), (0, 1, 1, 1), "own", 1, 1)
    put(2, (2, 0, 1, 0), (3, 0, 1, 0), "a", 0, 0)
    put(3, (2, 0, 1, 0), (3, 0, 1, 0), "b", 0, 1)
    put(2, (2, 0, 1, 1), (3, 0, 1, 1), "a", 0, 0)
    put(3, (2, 0, 1, 1), (1, 1, 0, 1), "own", 0, 1)
    for m in (2, 3):
        put(m, (1, 0, 0, 0), (0, 0, 1, m - 2), "own", 1, m - 2)
        put(m, (1, 0, 0, 1), (0, 1, 0, m - 2), "own", 0, m - 2)
    return rounds


KINDS = ("own", "x", "y", "a", "b")


def tables(nrow, ncol, rounds):
    ratio = ncol // nrow
    tight = (nrow, ncol) == (4, 8)
    out = []
    for i in range(nrow):
        for j in range(ncol):
            qs = []
            for m in range(nrow):
                if (i, j) in rounds[m]:
                    qs.append(rounds[m][i, j][2])
                elif tight:
                    qs.append(m ^ (2 * ((j >> 1) & 1)))
                else:
                    qs.append(m)
            masks = [((j * nrow + q) % ncol) ^ j for q in qs]
            sent = [-1] * nrow
            for m in range(nrow):
                for (frm, kind, _) in rounds[m].values():
                    if frm == (i, j):
                        sent[m] = KINDS.index(kind)
            late = int(tight and is_late((i, j)))
            out.append([i, j, int(i >= j // ratio), int(i == j // ratio), *qs, *masks, *sent, late, int(i > j // ratio)])
    return np.array(out, np.int32)


def is_late(to):
    return to in ((3, 0), (3, 2), (3, 4))


def local(nrow, ncol, front_diag, panel_rows, trailing, pattern):
    local_rows = trailing.shape[0]
    part = panel_rows.shape[0]
    half = nrow // 2
    everyone = [(i, j) for i in range(nrow) for j in range(ncol)]
    rounds = plan(nrow, ncol)
    info = jnp.asarray(tables(nrow, ncol, rounds))[lax.axis_index("row") * ncol + lax.axis_index("col")]
    piece_at, mask_at, sent_at, late_at = 4, 4 + nrow, 4 + 2 * nrow, 4 + 3 * nrow
    barrier = lax.optimization_barrier

    def across(x, mask):
        return lax.ppermute(x, AXES, [(i * ncol + j, i * ncol + (j ^ mask)) for i, j in everyone])

    def send(x, moves):
        return lax.ppermute(x, AXES, [(a * ncol + b, i * ncol + j) for (i, j), ((a, b), _, _) in moves.items()])

    tight = (nrow, ncol) == (4, 8)
    tile = min(BLOCK, part // 2 if tight else part)
    per = part // tile
    below_at = late_at + 1

    def fresh(m, *sources, ready=None):
        return piece_at + m, mask_at + m, late_at, sources, ready

    def cut(parts):
        return [(k, frm + s) for k, (_, _, size, _, frm) in enumerate(parts) for s in range(0, size, tile)]

    def stored(steps):
        return [(None, t * tile) for t in range(steps)]

    def change(pieces, parts, tiles, s, rows, near=0, needed=2, keeps=False, gives=False):
        return update(info, pattern, pieces, parts, tiles, near, needed, tile, part, cat, s, rows, keeps, gives)

    near = [m for m in range(2, ncol, 2) if not (tight and m == 6)]
    got = {m: across(panel_rows, m) for m in near}
    col = [send(panel_rows, rounds[m]) for m in range(half)]
    other = across(panel_rows, 1)
    diag_factor, inv, schur = factor(front_diag, trailing)
    panel_factor, cat = inverse(inv, panel_rows)
    held, cat = barrier(([panel_rows, other, *[got[m] for m in near], *col], cat))
    own, other, got, col = held[0], held[1], dict(zip(near, held[2:])), held[2 + len(near) :]

    if not tight:
        parts = [(0, 0, part, own, 0), (1, 0, part, other, 0)]
        for m in near:
            parts += [(m, 0, part, got[m], 0), (m + 1, 0, part, across(got[m], 1), 0)]
        col = [*col, *[send(own, rounds[m]) for m in range(half, nrow)]]
        parts.sort(key=lambda p: p[0])
        one, two = [[fresh(m, col[m]) for m in ms] for ms in (range(half), range(half, nrow))]
        schur, rows = change(one, parts, cut(parts), schur, None, keeps=True)
        schur, _ = change(two, parts, stored(ncol * per), schur, rows)
        return (diag_factor, panel_factor, schur)

    h = part // 2
    arrays = [own, got[2], got[4], col[0], col[1]]
    choices = [(k, 0) for k in range(5)]
    c_op, d_op, h1, h2 = pick(
        info,
        arrays,
        [
            [(0, part, choices, sent_at + 2)],
            [(0, part, choices, sent_at + 3)],
            [(0, h, [(1, 0)], None)],
            [(0, h, [(2, h)], None)],
        ],
    )
    c = send(c_op, rounds[2])
    d_early = send(d_op, {to: move for to, move in rounds[3].items() if not is_late(to)})
    got[3], got[5] = across(got[2], 1), across(got[4], 1)
    h1, h2 = across(h1, 4), across(h2, 2)
    parts = [(0, 0, part, own, 0), (1, 0, part, other, 0), (2, 0, part, got[2], 0)]
    parts += [(3, 0, part, got[3], 0), (4, 0, part, got[4], 0), (5, 0, part, got[5], 0)]
    schur, rows, ab = change([fresh(0, col[0]), fresh(1, col[1])], parts, cut(parts), schur, None, keeps=True, gives=True)
    d_op, schur = barrier((d_op, schur))
    d_late = send(d_op, {to: move for to, move in rounds[3].items() if is_late(to)})
    schur, rows, cc = change([fresh(2, c)], [], stored(6 * per), schur, rows, needed=below_at, gives=True)
    h1, h2, schur = barrier((h1, h2, schur))
    f1, f2 = across(h1, 1), across(h2, 1)
    far = [(6, 0, h, h1, 0), (6, h, h, h2, 0), (7, 0, h, f1, 0), (7, h, h, f2, 0)]
    beside = [p for p in parts if p[0] in (2, 3)]
    pieces = [(piece_at + m, None, None, (), (ab, m)) for m in (0, 1)]
    pieces += [fresh(2, ready=(cc, 0)), fresh(3, d_early, d_late)]
    schur, _ = change(pieces, far + beside, stored(6 * per) + cut(far), schur, rows, near=6 * per)
    return (diag_factor, panel_factor, schur)


def solution(mesh):
    nrow, ncol = mesh.shape["row"], mesh.shape["col"]
    return jax.shard_map(
        functools.partial(local, nrow, ncol),
        mesh=mesh,
        in_specs=(P(), P(("row", "col"), None), P("row", "col"), P("row", "col")),
        out_specs=(P(), P(("row", "col"), None), P("row", "col")),
        check_vma=False,
    )
```

time: 882 us -> 223 us (0.25); the launches traced: 868 us -> 220 us
  waiting for transfers between devices: 353 us -> 45.4 us
  other arithmetic: 271 us -> 0 us
  matrix products: 164 us -> 0 us
  Pallas kernels: 0 us -> 153 us
  local copies, waits for them, and re-layouts: 60.6 us -> 4.84 us
  between operations: 19.8 us -> 0.95 us
  starting transfers between devices: 0.08 us -> 15.8 us
    psum x1 -> x0, waiting for transfers between devices: 262 us -> none  [spread(): return lax.psum(block, axis)]
    another operation x33 -> x0, other arithmetic: 258 us -> none  [the longest x30 172 us: local(): diag_factor = jnp.linalg.cholesky(front_diag)]
    pallas_call x0 -> x6, Pallas kernels: none -> 153 us  [the longest x1 77.2 us: factor(): pl.pallas_call(factor_kernel, out_shape=(full, full, jax.ShapeDtypeStruct...]
    dot_general x1 -> x0, matrix products: 116 us -> none  [local(): update = jnp.dot(row_part, col_part.T, precision=lax.Precision.HIGHEST)]
    all_gather x1 -> x0, waiting for transfers between devices: 91.1 us -> none  [local(): row_part = lax.all_gather(panel_factor, 'col', axis=0, tiled=True)]
    another operation x29 -> x0, matrix products: 47.7 us -> none  [the longest x15 24.8 us: local(): jax.scipy.linalg.solve_triangular(diag_factor, panel_rows.T, lower=True)]
    ppermute x0 -> x14, waiting for transfers between devices: none -> 45.4 us  [the longest x9 26.7 us: across(): lax.ppermute(x, AXES, [(i * ncol + j, i * ncol + (j ^ mask)) for i, j in...]
    unnamed x13 -> x17, local copies, waits for them, and re-layouts: 32.7 us -> 3.56 us
  transfers between devices with their start and end apart: 2 -> 14, of which waited for: 2 -> 4; matrix products, arithmetic and copies ran while one was open for 3% -> 1% of each run, Pallas kernels for 0% -> 54%
where the time goes in v1:
time: 223 us; the launch traced here: 220 us
  Pallas kernels  153 us (69%)
  waiting for transfers between devices  45.4 us (20%)
  starting transfers between devices  15.8 us (7%)
  local copies, waits for them, and re-layouts  4.84 us (2%)
    pallas_call x1, Pallas kernels, factor(): pl.pallas_call(factor_kernel, out_shape=(full, full, jax.ShapeDtypeStruct...  77.2 us
    pallas_call x3, Pallas kernels, update(): pl.pallas_call(functools.partial(update_kernel, layout), out_shape=tuple(...  58.5 us
    ppermute x9, waiting for transfers between devices, across(): lax.ppermute(x, AXES, [(i * ncol + j, i * ncol + (j ^ mask)) for i, j in...  26.7 us
    ppermute x5, waiting for transfers between devices, send(): lax.ppermute(x, AXES, [(a * ncol + b, i * ncol + j) for (i, j), ((a, b),...  18.7 us
    pallas_call x1, Pallas kernels, inverse(): pl.pallas_call(inverse_kernel, out_shape=(jax.ShapeDtypeStruct((m, n), F3...  13.1 us
    ppermute x5, starting transfers between devices, send(): lax.ppermute(x, AXES, [(a * ncol + b, i * ncol + j) for (i, j), ((a, b),...  10.1 us
    ppermute x9, starting transfers between devices, across(): lax.ppermute(x, AXES, [(i * ncol + j, i * ncol + (j ^ mask)) for i, j in...  5.69 us
  transfers between devices with their start and end apart: 14, of which 4 were waited for; matrix products, arithmetic and copies ran while one was open for 1% of the time, Pallas kernels for 54%

profile of v1, /device:TPU:10, one launch (start us, length us, event | category | flops | bytes accessed | tf_op | source)
XLA Modules:
  0.0 220.1 jit_solution(17229446086262192170)
XLA Ops:
  0.6 3.6 %collective-permute-start.3 = (f32[512,1024]{1,0:T(8,128)}, f32[512,1024]{1,0:T(8,128)S(1)}, u32[]{:S(2)}, u32[]{:S(2)}) collective-permute-start(f32[512,1024]{1,0:T(8,128)} %refs_2_), channel_id=1, source_target_pairs={{1,8},{7,9},{2,16},{4,17},{10,18},{14,19},{0,24},{6,25},{8,26},{12... | collective-permute-start | bytes 6291464 | tf_op jit(solution)/shard_map/ppermute | solution.py:611
  4.3 1.0 collective-permute-start.2
  5.2 2.5 %collective-permute-start.1 = (f32[512,1024]{1,0:T(8,128)}, f32[512,1024]{1,0:T(8,128)S(1)}, u32[]{:S(2)}, u32[]{:S(2)}) collective-permute-start(f32[512,1024]{1,0:T(8,128)} %refs_2_), channel_id=1, source_target_pairs={{0,2},{1,3},{2,0},{3,1},{4,6},{5,7},{6,4},{7,5},{8,10},{9,11},{10,... | collective-permute-start | bytes 6291464 | tf_op jit(solution)/shard_map/ppermute | solution.py:608
  7.7 0.0 collective-permute-start
  7.7 2.0 collective-permute-start.4
  9.7 77.2 %factor.1 = (f32[1024,1024]{1,0:T(8,128)}, f32[1024,1024]{1,0:T(8,128)}, f32[4096,2048]{1,0:T(8,128)}) custom-call(f32[1024,1024]{1,0:T(8,128)} %a_ref.1, f32[4096,2048]{1,0:T(8,128)} %old_ref.1), custom_call_target="tpu_custom_call" | custom-call | flops 80000000000 | bytes 12582912 | tf_op jit(solution)/shard_map/factor/pallas_call | solution.py:139
  86.8 13.1 %inverse.1 = (f32[512,1024]{1,0:T(8,128)}, bf16[2048,1024]{1,0:T(8,128)(2,1)}) custom-call(f32[1024,1024]{1,0:T(8,128)} %get-tuple-element.32.inv_ref, f32[512,1024]{1,0:T(8,128)} %refs_2_), custom_call_target="tpu_custom_call" | custom-call | flops 8589934592 | bytes 16777216 | tf_op jit(solution)/shard_map/inverse/pallas_call | solution.py:185
  99.9 0.0 collective-permute-done.3.refs_3_.refs_0_
  99.9 0.0 copy-start.1
  99.9 0.0 collective-permute-done.2.refs_2_.refs_6_
  99.9 0.0 collective-permute-done.1.refs_1_.refs_4_.refs_9_
  100.0 0.0 copy-start
  100.0 0.0 collective-permute-done.refs_3_
  100.0 0.0 collective-permute-done.4.refs_4_.refs_1_
  100.0 1.3 copy-done.1
  101.2 1.1 collective-permute-start.7
  102.4 0.0 collective-permute-start.6
  102.4 1.3 dynamic-slice_bitcast_fusion.info
  103.7 0.0 copy-done
  103.7 0.0 copy-start.7
  103.7 4.4 %pick.1 = (f32[512,1024]{1,0:T(8,128)}, f32[512,1024]{1,0:T(8,128)}, f32[256,1024]{1,0:T(8,128)}, f32[256,1024]{1,0:T(8,128)}) custom-call(s32[18]{0:T(128)} %dynamic-slice_bitcast_fusion.info, f32[512,1024]{1,0:T(8,128)} %refs_2_, f32[512,1024]{1,0:T(8,128)} %copy-done, f32[512,1024]{1,0:T(8,128)} %collective-permute-done.2.refs_2_.refs_6_, ...), custom_call_target="tpu_custom_call" | custom-call | flops 1000 | bytes 1000 | tf_op jit(solution)/shard_map/pick/pallas_call | solution.py:229
  108.1 2.9 %collective-permute-start.9 = (f32[512,1024]{1,0:T(8,128)}, f32[512,1024]{1,0:T(8,128)}, u32[]{:S(2)}, u32[]{:S(2)}) collective-permute-start(f32[512,1024]{1,0:T(8,128)} %get-tuple-element.47), channel_id=1, source_target_pairs={{0,24},{1,25},{10,26},{11,27},{20,29},{21,28},{24,16},{25,17},{26,... | collective-permute-start | bytes 6291464 | tf_op jit(solution)/shard_map/ppermute | solution.py:611
  111.0 0.0 copy-done.7
  111.0 0.7 copy.15.pattern
  111.7 0.6 collective-permute-start.10
  112.3 0.0 collective-permute-start.11
  112.3 0.0 collective-permute-done.7.refs_7_
  112.3 0.8 collective-permute-start.5
  113.1 0.0 collective-permute-done.6.refs_5_.refs_10_
  113.1 23.1 %update.3 = (f32[4096,2048]{1,0:T(8,128)}, bf16[4096,2048]{1,0:T(8,128)(2,1)}, bf16[1024,2048]{1,0:T(8,128)(2,1)}) custom-call(s32[18]{0:T(128)} %dynamic-slice_bitcast_fusion.info, s32[16,8]{1,0:T(8,128)} %copy.15.pattern, f32[512,1024]{1,0:T(8,128)} %copy-done.1, ...), custom_call_target="tpu_custom_call", output_to_operand_aliasing={{0}: (11, {})} | custom-call | flops 1000 | bytes 1000 | tf_op jit(solution)/shard_map/update/pallas_call | solution.py:476
  136.2 0.8 collective-permute-start.8
  137.0 18.7 %collective-permute-done.9.refs_0_ = f32[512,1024]{1,0:T(8,128)} collective-permute-done((f32[512,1024]{1,0:T(8,128)}, f32[512,1024]{1,0:T(8,128)}, u32[]{:S(2)}, u32[]{:S(2)}) %collective-permute-start.9) | collective-permute-done | bytes 2097184 | tf_op jit(solution)/shard_map/ppermute | solution.py:611
  155.7 1.2 update.4
  156.9 0.0 collective-permute-done.10.refs_5_
  156.9 0.0 copy-start.4
  156.9 22.9 %collective-permute-done.11.refs_6_ = f32[256,1024]{1,0:T(8,128)} collective-permute-done((f32[256,1024]{1,0:T(8,128)}, f32[256,1024]{1,0:T(8,128)}, u32[]{:S(2)}, u32[]{:S(2)}) %collective-permute-start.11) | collective-permute-done | bytes 1048608 | tf_op jit(solution)/shard_map/ppermute | solution.py:608
  179.8 0.1 collective-permute-start.12
  179.9 0.4 collective-permute-start.13
  180.3 0.0 collective-permute-done.5.refs_0_
  180.3 0.0 copy-start.2
  180.3 2.4 %collective-permute-done.12.refs_7_ = f32[256,1024]{1,0:T(8,128)S(1)} collective-permute-done((f32[256,1024]{1,0:T(8,128)S(1)}, f32[256,1024]{1,0:T(8,128)S(1)}, u32[]{:S(2)}, u32[]{:S(2)}) %collective-permute-start.12) | collective-permute-done | bytes 1048608 | tf_op jit(solution)/shard_map/ppermute | solution.py:608
  182.8 0.0 copy-start.5
  182.8 1.4 collective-permute-done.13.refs_8_
  184.2 0.0 copy-start.6
  184.2 0.0 collective-permute-done.8.refs_1_
  184.2 0.0 copy-done.5
  184.2 0.0 copy-start.3
  184.2 1.0 copy-done.6
  185.2 0.0 copy-done.4
  185.2 0.0 copy-done.2
  185.2 0.6 copy-done.3
  185.8 34.1 %update.5 = (f32[4096,2048]{1,0:T(8,128)}, bf16[4096,2048]{1,0:T(8,128)(2,1)}) custom-call(s32[18]{0:T(128)} %dynamic-slice_bitcast_fusion.info, s32[16,8]{1,0:T(8,128)} %copy.15.pattern, f32[512,1024]{1,0:T(8,128)} %copy-done.2, f32[512,1024]{1,0:T(8,128)} %copy-done.3, ...), custom_call_target="tpu_custom_call", output_to_operand_aliasing={{0}: (14, {}), {1}: (15, {})} | custom-call | flops 1000 | bytes 1000 | tf_op jit(solution)/shard_map/update/pallas_call | solution.py:476
Async XLA Ops:
  0.6 99.3 %collective-permute-start.3 = (f32[512,1024]{1,0:T(8,128)}, f32[512,1024]{1,0:T(8,128)S(1)}, u32[]{:S(2)}, u32[]{:S(2)}) collective-permute-start(f32[512,1024]{1,0:T(8,128)} %refs_2_), channel_id=1, source_target_pairs={{1,8},{7,9},{2,16},{4,17},{10,18},{14,19},{0,24},{6,25},{8,26},{12... | collective-permute-start | bytes 6291464 | tf_op jit(solution)/shard_map/ppermute | solution.py:611
  4.3 95.7 %collective-permute-start.2 = (f32[512,1024]{1,0:T(8,128)}, f32[512,1024]{1,0:T(8,128)}, u32[]{:S(2)}, u32[]{:S(2)}) collective-permute-start(f32[512,1024]{1,0:T(8,128)} %refs_2_), channel_id=1, source_target_pairs={{0,4},{1,5},{2,6},{3,7},{4,0},{5,1},{6,2},{7,3},{8,12},{9,13},{10,... | collective-permute-start | bytes 6291464 | tf_op jit(solution)/shard_map/ppermute | solution.py:608
  5.2 94.7 %collective-permute-start.1 = (f32[512,1024]{1,0:T(8,128)}, f32[512,1024]{1,0:T(8,128)S(1)}, u32[]{:S(2)}, u32[]{:S(2)}) collective-permute-start(f32[512,1024]{1,0:T(8,128)} %refs_2_), channel_id=1, source_target_pairs={{0,2},{1,3},{2,0},{3,1},{4,6},{5,7},{6,4},{7,5},{8,10},{9,11},{10,... | collective-permute-start | bytes 6291464 | tf_op jit(solution)/shard_map/ppermute | solution.py:608
  7.7 92.3 %collective-permute-start = (f32[512,1024]{1,0:T(8,128)}, f32[512,1024]{1,0:T(8,128)}, u32[]{:S(2)}, u32[]{:S(2)}) collective-permute-start(f32[512,1024]{1,0:T(8,128)} %refs_2_), channel_id=1, source_target_pairs={{0,1},{1,0},{2,3},{3,2},{4,5},{5,4},{6,7},{7,6},{8,9},{9,8},{10,11... | collective-permute-start | bytes 6291464 | tf_op jit(solution)/shard_map/ppermute | solution.py:608
  7.7 92.3 %collective-permute-start.4 = (f32[512,1024]{1,0:T(8,128)}, f32[512,1024]{1,0:T(8,128)}, u32[]{:S(2)}, u32[]{:S(2)}) collective-permute-start(f32[512,1024]{1,0:T(8,128)} %refs_2_), channel_id=1, source_target_pairs={{0,8},{6,9},{3,16},{5,17},{11,18},{15,19},{1,24},{7,25},{9,26},{13... | collective-permute-start | bytes 6291464 | tf_op jit(solution)/shard_map/ppermute | solution.py:611
  99.9 1.3 copy-start.1
  100.0 3.7 %copy-start = (f32[512,1024]{1,0:T(8,128)}, f32[512,1024]{1,0:T(8,128)S(1)}, u32[]{:S(2)}) copy-start(f32[512,1024]{1,0:T(8,128)S(1)} %collective-permute-done.1.refs_1_.refs_4_.refs_9_) | copy-start | bytes 6291460
  101.2 11.0 %collective-permute-start.7 = (f32[512,1024]{1,0:T(8,128)}, f32[512,1024]{1,0:T(8,128)}, u32[]{:S(2)}, u32[]{:S(2)}) collective-permute-start(f32[512,1024]{1,0:T(8,128)} %collective-permute-done.2.refs_2_.refs_6_), channel_id=1, source_target_pairs={{0,1},{1,0},{2,3},{3,2},{4,5},{5,4},{6,7},{7,6},{8,9},{9,8},{10,11... | collective-permute-start | bytes 6291464 | tf_op jit(solution)/shard_map/ppermute | solution.py:608
  102.4 10.7 %collective-permute-start.6 = (f32[512,1024]{1,0:T(8,128)S(1)}, f32[512,1024]{1,0:T(8,128)}, u32[]{:S(2)}, u32[]{:S(2)}) collective-permute-start(f32[512,1024]{1,0:T(8,128)S(1)} %collective-permute-done.1.refs_1_.refs_4_.refs_9_), channel_id=1, source_target_pairs={{0,1},{1,0},{2,3},{3,2},{4,5},{5,4},{6,7},{7,6},{8,9},{9,8},{10,11... | collective-permute-start | bytes 6291464 | tf_op jit(solution)/shard_map/ppermute | solution.py:608
  103.7 7.3 %copy-start.7 = (s32[16,8]{0,1:T(8,128)S(1)}, s32[16,8]{0,1:T(8,128)}, u32[]{:S(2)}) copy-start(s32[16,8]{0,1:T(8,128)} %param.8) | copy-start | bytes 1540
  108.1 47.6 %collective-permute-start.9 = (f32[512,1024]{1,0:T(8,128)}, f32[512,1024]{1,0:T(8,128)}, u32[]{:S(2)}, u32[]{:S(2)}) collective-permute-start(f32[512,1024]{1,0:T(8,128)} %get-tuple-element.47), channel_id=1, source_target_pairs={{0,24},{1,25},{10,26},{11,27},{20,29},{21,28},{24,16},{25,17},{26,... | collective-permute-start | bytes 6291464 | tf_op jit(solution)/shard_map/ppermute | solution.py:611
  111.7 45.2 %collective-permute-start.10 = (f32[256,1024]{1,0:T(8,128)}, f32[256,1024]{1,0:T(8,128)S(1)}, u32[]{:S(2)}, u32[]{:S(2)}) collective-permute-start(f32[256,1024]{1,0:T(8,128)} %get-tuple-element.51), channel_id=1, source_target_pairs={{0,4},{1,5},{2,6},{3,7},{4,0},{5,1},{6,2},{7,3},{8,12},{9,13},{10,... | collective-permute-start | bytes 3145736 | tf_op jit(solution)/shard_map/ppermute | solution.py:608
  112.3 67.5 %collective-permute-start.11 = (f32[256,1024]{1,0:T(8,128)}, f32[256,1024]{1,0:T(8,128)}, u32[]{:S(2)}, u32[]{:S(2)}) collective-permute-start(f32[256,1024]{1,0:T(8,128)} %get-tuple-element.52), channel_id=1, source_target_pairs={{0,2},{1,3},{2,0},{3,1},{4,6},{5,7},{6,4},{7,5},{8,10},{9,11},{10,... | collective-permute-start | bytes 3145736 | tf_op jit(solution)/shard_map/ppermute | solution.py:608
  112.3 68.1 %collective-permute-start.5 = (f32[512,1024]{1,0:T(8,128)}, f32[512,1024]{1,0:T(8,128)S(1)}, u32[]{:S(2)}, u32[]{:S(2)}) collective-permute-start(f32[512,1024]{1,0:T(8,128)} %get-tuple-element.45), channel_id=1, source_target_pairs={{6,25},{14,27},{23,29},{24,16},{7,17},{26,18},{13,19},{3,8},{5,9}} | collective-permute-start | bytes 6291464 | tf_op jit(solution)/shard_map/ppermute | solution.py:611
  136.2 48.0 %collective-permute-start.8 = (f32[512,1024]{1,0:T(8,128)}, f32[512,1024]{1,0:T(8,128)S(1)}, u32[]{:S(2)}, u32[]{:S(2)}) collective-permute-start(f32[512,1024]{1,0:T(8,128)} %get-tuple-element.45), channel_id=1, source_target_pairs={{1,24},{11,26},{20,28}} | collective-permute-start | bytes 6291464 | tf_op jit(solution)/shard_map/ppermute | solution.py:611
  156.9 28.3 %copy-start.4 = (f32[256,1024]{1,0:T(8,128)}, f32[256,1024]{1,0:T(8,128)S(1)}, u32[]{:S(2)}) copy-start(f32[256,1024]{1,0:T(8,128)S(1)} %collective-permute-done.10.refs_5_) | copy-start | bytes 3145732
  179.8 2.9 %collective-permute-start.12 = (f32[256,1024]{1,0:T(8,128)S(1)}, f32[256,1024]{1,0:T(8,128)S(1)}, u32[]{:S(2)}, u32[]{:S(2)}) collective-permute-start(f32[256,1024]{1,0:T(8,128)S(1)} %collective-permute-done.10.refs_5_), channel_id=1, source_target_pairs={{0,1},{1,0},{2,3},{3,2},{4,5},{5,4},{6,7},{7,6},{8,9},{9,8},{10,11... | collective-permute-start | bytes 3145736 | tf_op jit(solution)/shard_map/ppermute | solution.py:608
  179.9 4.2 %collective-permute-start.13 = (f32[256,1024]{1,0:T(8,128)}, f32[256,1024]{1,0:T(8,128)S(1)}, u32[]{:S(2)}, u32[]{:S(2)}) collective-permute-start(f32[256,1024]{1,0:T(8,128)} %collective-permute-done.11.refs_6_), channel_id=1, source_target_pairs={{0,1},{1,0},{2,3},{3,2},{4,5},{5,4},{6,7},{7,6},{8,9},{9,8},{10,11... | collective-permute-start | bytes 3145736 | tf_op jit(solution)/shard_map/ppermute | solution.py:608
  180.3 4.9 %copy-start.2 = (f32[512,1024]{1,0:T(8,128)}, f32[512,1024]{1,0:T(8,128)S(1)}, u32[]{:S(2)}) copy-start(f32[512,1024]{1,0:T(8,128)S(1)} %collective-permute-done.5.refs_0_) | copy-start | bytes 6291460
  182.8 1.4 copy-start.5
  184.2 1.0 copy-start.6
  184.2 1.6 copy-start.3
